TPU v7x, 32 devices: a whole 2x2x4 slice. The times are simulated.
32 devices in a mesh: groups: 2 (over x), tiles: 8 (over z, y), sub: 2 (over core).
Axes of the slice: x: 2, y: 2, z: 4, core: 2. Of those that a mesh axis runs over, the one named last changes fastest.
Arguments:
- density: float32 [768, 1536], P(('groups', 'tiles'), 'sub'), parts along dimension 0, may hold values from 0.8 to 1.2
- momentum: float32 [3, 768, 1536], P(None, ('groups', 'tiles'), 'sub'), parts along dimension 1, may hold values from -0.4 to 0.4
- stress: float32 [6, 768, 1536], P(None, ('groups', 'tiles'), 'sub'), parts along dimension 1, may hold values from -0.4 to 0.4
- red_density: float32 [768, 1536], P(('groups', 'tiles'), 'sub'), parts along dimension 0, may hold values from 0.1 to 0.8
- solid: int32 [768, 1536], P(('groups', 'tiles'), 'sub'), parts along dimension 0, may hold values 0 or 1
- widths: int32 [16], P('groups'), parts along dimension 0, may hold values from 1 to 3, 16 in all
Outputs:
- density_next: float32 [768, 1536], P(('groups', 'tiles'), 'sub'), parts along dimension 0
- momentum_next: float32 [3, 768, 1536], P(None, ('groups', 'tiles'), 'sub'), parts along dimension 1
- stress_next: float32 [6, 768, 1536], P(None, ('groups', 'tiles'), 'sub'), parts along dimension 1
- red_next: float32 [768, 1536], P(('groups', 'tiles'), 'sub'), parts along dimension 0
There are 2 independent parts, one for each index of `groups`. A program takes and returns all parts, laid end to end along the dimension named above; each array names one. Nothing has to cross between parts.
Inputs may be any that keep to these rules, and one draw needn't show every extreme that they name: Device k along tiles owns the tile columns from widths[0] + ... + widths[k-1] on, widths[k] of them, alike in every part of sub; they sum to 16, and one equals 3. 1 marks a solid cell, 0 a pore cell.
All inputs are finite; a program needn't handle non-finite values. No bound on the sum of `solid` on one device may be relied on, other than what follows from the above.
Results may differ from a plain program's by a relative error of at most 0.0003.
Values sent between devices are 32-bit elements; how exact they have to be, the bound alone decides.
No kernel may reach another device: no remote copies, remote signals or barrier semaphores. Data moves between devices by JAX's collectives and lax.ppermute only.
A program may use at most 64 MiB of HBM per device.

v0:
```python
import functools

import jax
import jax.numpy as jnp
from jax import lax
from jax.experimental import pallas as pl
from jax.experimental.pallas import tpu as pltpu
from jax.sharding import PartitionSpec as P

TILE = 16
STEPS = 2
RELAX_TIME = 0.8
SURFACE = 0.1
SEPARATION = 0.7

LANES = 128
SUBLANES = 8
FULL = 3
HALO = FULL + 1
FIELDS = 11
PLANES = FIELDS + 1
MOVED = 19
REDS = 5
RIM = 4
SLAB = HALO + 2 * RIM
OWN_TILES = SUBLANES - 2
GROUP = 4
PACKED = FULL * PLANES // GROUP * (GROUP - 1)
END_ROWS = (PACKED + 1) * SUBLANES
HALF = LANES // 2
PAIRS = PLANES // 2
KEPT = 2
COLOUR_BLOCK = (8, 1)
COLLIDE_BLOCK = (2, 4)
ARRIVE_BLOCK = (8, 1)
VMEM = pl.BlockSpec(memory_space=pltpu.VMEM)
SMEM = pl.BlockSpec(memory_space=pltpu.SMEM)
ANY = pl.BlockSpec(memory_space=pl.ANY)
HBM = pl.BlockSpec(memory_space=pltpu.HBM)


class Rows:
    def __init__(self, parts):
        self.parts = parts

    def _with(self, other, operation):
        others = other.parts if isinstance(other, Rows) else [other] * len(self.parts)
        return Rows([operation(one, two) for one, two in zip(self.parts, others)])

    def __add__(self, other):
        return self._with(other, lambda one, two: one + two)

    def __sub__(self, other):
        return self._with(other, lambda one, two: one - two)

    def __rsub__(self, other):
        return self._with(other, lambda one, two: two - one)

    def __mul__(self, other):
        return self._with(other, lambda one, two: one * two)

    def __or__(self, other):
        return self._with(other, lambda one, two: one | two)

    def __eq__(self, other):
        return self._with(other, lambda one, two: one == two)

    __radd__, __rmul__, __ror__ = __add__, __mul__, __or__

    def each(self, operation):
        return Rows([operation(part) for part in self.parts])


def select(mask, yes, no):
    count = max(len(item.parts) for item in (mask, yes, no) if isinstance(item, Rows))
    columns = [
        item.parts if isinstance(item, Rows) else [item] * count for item in (mask, yes, no)
    ]
    return Rows([jnp.where(*row) for row in zip(*columns)])


def roll_lanes(values, amount):
    return values.each(lambda part: pltpu.roll(part, amount % LANES, 1))


def roll_sublanes(values, amount):
    return values.each(lambda part: pltpu.roll(part, amount % SUBLANES, 0))


class Geometry:
    def __init__(self, info, own_tiles):
        live, first, last, sub_index = info[0], info[1], info[2], info[3]
        self.live = live
        self.low_row = jnp.where(first == 1, 0, -1000)
        self.high_row = jnp.where(last == 1, live, 1000)
        shape = (SUBLANES, LANES)
        lane = lax.broadcasted_iota(jnp.int32, shape, 1)
        tile = lax.broadcasted_iota(jnp.int32, shape, 0)
        depth = lane & (TILE - 1)
        low_part = sub_index == 0
        high_part = sub_index == 1
        z_walls = {1: depth == 0, -1: depth == TILE - 1}
        y_walls = {
            1: (tile == 1) & (lane < TILE) & low_part,
            -1: (tile == own_tiles) & (lane >= LANES - TILE) & high_part,
        }
        self.walls = {(0, vel_z): wall for vel_z, wall in z_walls.items()}
        for vel_y, y_wall in y_walls.items():
            self.walls[vel_y, 0] = y_wall
            for vel_z, z_wall in z_walls.items():
                self.walls[vel_y, vel_z] = y_wall | z_wall
        own = (tile >= 1) & (tile <= own_tiles)
        self.domain = own | ((tile == own_tiles + 1) & low_part) | ((tile == 0) & high_part)
        self.first_lanes = lane < TILE
        self.last_lanes = lane >= LANES - TILE

    def from_low_y(self, values):
        return roll_lanes(select(self.last_lanes, roll_sublanes(values, 1), values), TILE)

    def from_high_y(self, values):
        return roll_lanes(select(self.first_lanes, roll_sublanes(values, -1), values), -TILE)

    def from_low_z(self, values):
        return select(self.walls[0, 1], 0.0, roll_lanes(values, 1))

    def from_high_z(self, values):
        return select(self.walls[0, -1], 0.0, roll_lanes(values, -1))


def flat_rows(row, count, tile_offset=0):
    start = row * SUBLANES
    if not isinstance(start, int):
        start = pl.multiple_of(start, SUBLANES)
    return pl.ds(start + tile_offset, count * SUBLANES)


class Block:
    def __init__(self, geometry, spans, inner=False, store_rows=None):
        self.spans = spans
        self.store_rows = store_rows or [local for row, local, count in spans]
        rows = [row + extra for row, local, count in spans for extra in range(count)]
        self.inner = inner
        rows = [row + extra for row, local, count in spans for extra in range(count)]
        if inner:
            self.x_walls = {}
            self.valid = geometry.domain
            self.kinds = [0]
            return
        ids = Rows([row + jnp.zeros((SUBLANES, LANES), jnp.int32) for row in rows])
        self.x_walls = {1: ids == geometry.low_row, -1: ids == geometry.high_row - 1}
        self.valid = ids.each(
            lambda part: geometry.domain & (part >= geometry.low_row) & (part < geometry.high_row)
        )
        self.kinds = [
            jnp.where(row == geometry.low_row, 1, 0) + jnp.where(row == geometry.high_row - 1, 2, 0)
            for row in rows
        ]

    def load(self, ref, index, offset=0):
        return Rows([
            ref[index, flat_rows(local + offset + extra, 1), :]
            for row, local, count in self.spans
            for extra in range(count)
        ])

    def store(self, ref, index, values):
        targets = [
            target + extra
            for (row, local, count), target in zip(self.spans, self.store_rows)
            for extra in range(count)
        ]
        for target, part in zip(targets, values.parts):
            ref[index, flat_rows(target, 1), :] = part

    def store_crossed(self, geometry, ref, index, vel_y, values):
        mask = geometry.last_lanes if vel_y == 1 else geometry.first_lanes
        rows = [local + extra for row, local, count in self.spans for extra in range(count)]
        for row, part in zip(rows, values.parts):
            ref[index, flat_rows(row, 1), :] = part
            pltpu.store(ref.at[index, flat_rows(row, 1, vel_y), :], part, mask=mask)

    def wall_terms(self, walls, position):
        terms = [walls[position, flat_rows(kind, 1), :] for kind in self.kinds]
        return terms[0] if self.inner else Rows(terms)


def fill_wall_table(walls, geometry):
    one = jnp.ones((SUBLANES, LANES), jnp.float32)
    up_y, down_y, up_z, down_z = [
        jnp.where(geometry.walls[key], 0.0, one) for key in ((-1, 0), (1, 0), (0, -1), (0, 1))
    ]
    sum_y, sum_z = up_y + down_y, up_z + down_z
    for kind, (up_x, down_x) in enumerate(((1.0, 1.0), (1.0, 0.0), (0.0, 1.0))):
        sum_x = up_x + down_x
        around_x = 2.0 + sum_y + sum_z
        total = 12.0 + 2.0 * (sum_x + sum_y + sum_z) + sum_x * (sum_y + sum_z) + sum_y * sum_z
        rows = (
            (up_x - down_x) * around_x,
            (up_y - down_y) * (2.0 + sum_x + sum_z),
            (up_z - down_z) * (2.0 + sum_x + sum_y),
            36.0 - total,
        )
        for position, row in enumerate(rows):
            walls[position, flat_rows(kind, 1), :] = row


VELOCITIES = tuple(
    tuple(sign if axis == place else 0 for place in range(3)) for axis in range(3) for sign in (1, -1)
) + tuple(
    tuple({a: one, b: two}.get(place, 0) for place in range(3))
    for a, b in ((0, 1), (0, 2), (1, 2))
    for one, two in ((1, 1), (-1, -1), (1, -1), (-1, 1))
)
VELOCITIES = ((0, 0, 0),) + VELOCITIES
SIDEWAYS = tuple(place for place, velocity in enumerate(VELOCITIES) if velocity[1] != 0)
CROSSED = len(SIDEWAYS)


def colour_stage(block, geometry, fields, colours):
    density = block.load(fields, 0)
    red = block.load(fields, 10)
    colour = select(block.valid, 2.0 * red - density, 0.0)
    along_y = geometry.from_low_y(colour) + geometry.from_high_y(colour)
    along_z = geometry.from_low_z(colour) + geometry.from_high_z(colour)
    block.store(colours, 0, colour)
    block.store(colours, 1, 2.0 * colour + (along_y + along_z))
    block.store(colours, 2, along_y)
    block.store(colours, 3, along_z)


def collide_stage(block, geometry, fields, solids, colours, walls, state):
    relaxing = 1.0 - 1.0 / RELAX_TIME
    third = 1.0 / 3.0
    colour = block.load(colours, 0)
    doubled = 2.0 * colour + (block.load(colours, 0, -1) + block.load(colours, 0, 1))
    term_y = doubled + block.load(colours, 3)
    term_z = doubled + block.load(colours, 2)
    grad_x = block.load(colours, 1, 1) - block.load(colours, 1, -1)
    grad_y = geometry.from_high_y(term_y) - geometry.from_low_y(term_y)
    grad_z = geometry.from_high_z(term_z) - geometry.from_low_z(term_z)
    if not block.inner:
        grad_x = grad_x - block.wall_terms(walls, 0) * colour
    grad_y = grad_y - block.wall_terms(walls, 1) * colour
    grad_z = grad_z - block.wall_terms(walls, 2) * colour

    fluid = block.load(solids, PLANES - 1) == 0.0
    density = block.load(fields, 0)
    red = block.load(fields, 10)
    flux = [block.load(fields, 1 + axis) for axis in range(3)]
    stress = [block.load(fields, 4 + part) for part in range(6)]
    square_xx, square_yy, square_zz = grad_x * grad_x, grad_y * grad_y, grad_z * grad_z
    square = square_xx + square_yy + square_zz
    inverse = select(fluid, (1.0 + square * (1.0 / 144.0)).each(lax.rsqrt), 0.0)
    trace = third * square
    strength = (SURFACE / (8.0 * 144.0)) * inverse
    keep = select(fluid, relaxing / 8.0, 1.0 / 8.0)
    eighths = [0.125 * part for part in flux]
    own = [
        eighths[axis] * flux[axis] + (keep * stress[axis] + strength * (squared - trace))
        for axis, squared in enumerate((square_xx, square_yy, square_zz))
    ]
    strength, keep = 2.0 * strength, 2.0 * keep
    quarters = [2.0 * part for part in eighths[:2]]
    grads = (grad_x, grad_y, grad_z)
    cross = [
        quarters[a] * flux[b] + (keep * stress[3 + plane] + strength * (grads[a] * grads[b]))
        for plane, (a, b) in enumerate(((0, 1), (0, 2), (1, 2)))
    ]
    base = density * (1.0 / 36.0) - third * (own[0] + own[1] + own[2])
    sign = select(fluid, 1.0 / 12.0, -1.0 / 12.0)
    run = [sign * part for part in flux]
    mixing = ((SEPARATION / 144.0) * red) * ((density - red) * inverse)
    red_run = [0.5 * part + mixing * grad for part, grad in zip(run, grads)]
    moved, reds, crossed = state

    def leave(direction, values):
        block.store(moved, direction, values)
        if direction in SIDEWAYS:
            place = SIDEWAYS.index(direction)
            block.store_crossed(geometry, crossed, place, VELOCITIES[direction][1], values)

    leave(0, 12.0 * base)
    straight = [base + part for part in own]
    for axis in range(3):
        middle = 2.0 * straight[axis]
        swing = 2.0 * run[axis]
        leave(1 + 2 * axis, middle + swing)
        leave(2 + 2 * axis, middle - swing)
    for plane, (a, b) in enumerate(((0, 1), (0, 2), (1, 2))):
        middle = straight[a] + own[b]
        same, other = middle + cross[plane], middle - cross[plane]
        along, against = run[a] + run[b], run[a] - run[b]
        first = 7 + 4 * plane
        leave(first, same + along)
        leave(first + 1, same - along)
        leave(first + 2, other + against)
        leave(first + 3, other - against)

    red_base = select(block.valid, red * (1.0 / 36.0), 0.0)
    red_run = [select(block.valid, part, 0.0) for part in red_run]
    block.store(reds, 0, red_base)
    block.store(reds, 1, red_base + red_run[0])
    block.store(reds, 2, red_base - red_run[0])
    block.store(reds, 3, red_run[1])
    block.store(reds, 4, red_run[2])


def arrive_stage(block, geometry, walls, state, fields):
    third = 1.0 / 3.0
    moved, reds, crossed = state
    own = [None] * MOVED

    def here(direction):
        if own[direction] is None:
            own[direction] = block.load(moved, direction)
        return own[direction]

    def arrived(direction, opposite):
        vel_x, vel_y, vel_z = VELOCITIES[direction]
        if vel_y != 0:
            values = block.load(crossed, SIDEWAYS.index(direction), -vel_x)
        else:
            values = here(direction) if vel_x == 0 else block.load(moved, direction, -vel_x)
        if vel_y != 0 or vel_z != 0:
            values = roll_lanes(values, TILE * vel_y + vel_z)
        masks = []
        if vel_x in block.x_walls:
            masks.append(block.x_walls[vel_x])
        if (vel_y, vel_z) in geometry.walls:
            masks.append(geometry.walls[vel_y, vel_z])
        if not masks:
            return values
        wall = functools.reduce(lambda one, two: one | two, masks)
        return select(wall, here(opposite), values)

    red = block.load(reds, 0)
    red_y = block.load(reds, 3)
    red_z = block.load(reds, 4)
    from_x = block.load(reds, 1, -1) + block.load(reds, 2, 1)
    spread = 2.0 * red + from_x
    spread_y = 2.0 * red_y + (block.load(reds, 3, -1) + block.load(reds, 3, 1))
    spread_z = 2.0 * red_z + (block.load(reds, 4, -1) + block.load(reds, 4, 1))
    up_y, down_y = red + red_y, red - red_y
    low_y = (
        (spread + spread_y)
        + geometry.from_low_z(up_y + red_z)
        + geometry.from_high_z(up_y - red_z)
    )
    high_y = (
        (spread - spread_y)
        + geometry.from_low_z(down_y + red_z)
        + geometry.from_high_z(down_y - red_z)
    )
    bounced = (
        block.wall_terms(walls, 3) * red
        - block.wall_terms(walls, 1) * red_y
        - block.wall_terms(walls, 2) * red_z
    )
    if not block.inner:
        bounced = bounced - block.wall_terms(walls, 0) * (block.load(reds, 1) - red)
    red_total = (
        12.0 * red
        + 2.0 * from_x
        + geometry.from_low_z(spread + spread_z)
        + geometry.from_high_z(spread - spread_z)
        + geometry.from_low_y(low_y)
        + geometry.from_high_y(high_y)
        + bounced
    )
    rest = here(0)
    sums, diffs = [], []
    for axis in range(3):
        up = arrived(1 + 2 * axis, 2 + 2 * axis)
        down = arrived(2 + 2 * axis, 1 + 2 * axis)
        sums.append(up + down)
        diffs.append(up - down)
    total = rest + sums[0] + sums[1] + sums[2]
    cross = []
    for plane, (a, b) in enumerate(((0, 1), (0, 2), (1, 2))):
        first = 7 + 4 * plane
        parts = [arrived(first + offset, first + (offset ^ 1)) for offset in range(4)]
        same, other = parts[0] + parts[1], parts[2] + parts[3]
        along, against = parts[0] - parts[1], parts[2] - parts[3]
        both = same + other
        cross.append(same - other)
        total = total + both
        sums[a], sums[b] = sums[a] + both, sums[b] + both
        diffs[a], diffs[b] = diffs[a] + (along + against), diffs[b] + (along - against)
    shared = third * total
    block.store(fields, 0, total)
    for axis in range(3):
        block.store(fields, 1 + axis, diffs[axis])
        block.store(fields, 4 + axis, sums[axis] - shared - diffs[axis] * diffs[axis])
    for plane, (a, b) in enumerate(((0, 1), (0, 2), (1, 2))):
        block.store(fields, 7 + plane, cross[plane] - diffs[a] * diffs[b])
    block.store(fields, 10, red_total)


def over_rows(geometry, first, size, blocks, stage):
    trip = size * blocks
    rest = -2 * first % trip
    assert TILE % trip == 0 and rest % min(size, rest or size) == 0

    def run(start, count, step_size):
        for offset in range(0, count, step_size):
            row = start + offset
            stage(Block(geometry, [(row, row, step_size)], inner=True))

    def step(index, carry):
        run(first + index * trip, trip, size)
        return carry

    trips = (geometry.live - 2 * first - rest) // trip
    lax.fori_loop(0, trips, step, 0)
    if rest:
        run(geometry.live - first - rest, rest, min(size, rest))


def block_tiles():
    return lax.broadcasted_iota(jnp.int32, (SUBLANES, LANES), 0)


def roll_tiles(block, amount):
    return pltpu.roll(block, amount % SUBLANES, 0)


def pack_blocks(blocks):
    tiles, rest = block_tiles(), blocks[GROUP - 1]
    packed = []
    for number, block in enumerate(blocks[: GROUP - 1]):
        low, high = 2 * number + 1, 2 * number + 2
        block = jnp.where(tiles == 0, roll_tiles(rest, -low), block)
        packed.append(jnp.where(tiles == SUBLANES - 1, roll_tiles(rest, SUBLANES - 1 - high), block))
    return packed


def unpack_blocks(packed):
    tiles, rest = block_tiles(), None
    for number, block in enumerate(packed):
        low, high = 2 * number + 1, 2 * number + 2
        part = jnp.where(tiles == low, roll_tiles(block, low), roll_tiles(block, high - SUBLANES + 1))
        rest = part if rest is None else jnp.where(tiles >= low, part, rest)
    return list(packed) + [rest]


def spread_tile(raw, raw_solid, index, row, target, target_row):
    source = raw_solid if index == FIELDS else raw.at[index]
    for tile in range(OWN_TILES):
        values = source[pl.ds(row, SUBLANES), pl.ds(tile * LANES, LANES)].astype(jnp.float32)
        start = target_row * SUBLANES + 1 + tile
        target[index, pl.ds(start, SUBLANES, stride=SUBLANES), :] = values


def load_kernel(
    tiles_count, density, momentum, stress, red, solid, widths,
    info, raw, raw_solid, packet, mine,
    first_tile, last_tile, held_widths, sems,
):
    row_count, flat_count = raw_solid.shape
    own_tiles = flat_count // LANES
    copies = [
        pltpu.make_async_copy(widths, held_widths, sems.at[0]),
        pltpu.make_async_copy(density, raw.at[0], sems.at[1]),
        pltpu.make_async_copy(momentum, raw.at[pl.ds(1, 3)], sems.at[2]),
        pltpu.make_async_copy(red, raw.at[10], sems.at[3]),
        pltpu.make_async_copy(solid, raw_solid, sems.at[4]),
        pltpu.make_async_copy(stress.at[pl.ds(0, 3)], raw.at[pl.ds(4, 3)], sems.at[5]),
        pltpu.make_async_copy(stress.at[pl.ds(3, 3)], raw.at[pl.ds(7, 3)], sems.at[6]),
    ]
    for copy in copies:
        copy.start()
    tiles_index, sub_index = lax.axis_index("tiles"), lax.axis_index("sub")
    low_part = sub_index == 0
    edge_start = pl.multiple_of(jnp.where(low_part, (own_tiles - 1) * LANES, 0), LANES)

    copies[0].wait()
    live = held_widths[tiles_index] * TILE
    info[0] = live
    info[1] = (tiles_index == 0).astype(jnp.int32)
    info[2] = (tiles_index == tiles_count - 1).astype(jnp.int32)
    info[3] = sub_index

    near_cut = lax.broadcasted_iota(jnp.int32, (SUBLANES, LANES), 1) < HALF
    near_cut = near_cut == jnp.logical_not(low_part)
    near_last = pl.multiple_of(live - SUBLANES, SUBLANES)
    ready = {0: copies[1], 1: copies[2], 10: copies[3], 11: copies[4], 4: copies[5], 7: copies[6]}
    for index in (0, 1, 2, 3, 10, 11, 4, 5, 6, 7, 8, 9):
        if index in ready:
            ready[index].wait()
        for target, row in ((first_tile, 0), (last_tile, near_last)):
            spread_tile(raw, raw_solid, index, row, target, 0)

    edges = pl.ds(edge_start, LANES)
    for pair in range(PAIRS):
        later = raw_solid if pair + PAIRS == FIELDS else raw.at[pair + PAIRS]
        for row in range(0, row_count, SUBLANES):
            rows = pl.ds(row, SUBLANES)
            beside = pltpu.roll(later[rows, edges].astype(jnp.float32), HALF, 1)
            both = jnp.where(near_cut, raw[pair, rows, edges], beside)
            packet[pl.ds(pair * row_count + row, SUBLANES), :] = both

    after = PAIRS * row_count
    ends = ((packet, after, jnp.logical_not(low_part)), (mine, 0, low_part))
    for target, at, use_last in ends:
        def row_of(index, number_first, number_last):
            first = first_tile[index, flat_rows(number_first, 1), :]
            last = last_tile[index, flat_rows(number_last, 1), :]
            return jnp.where(use_last, last, first)

        place = pl.ds(at + PACKED * SUBLANES, SUBLANES)
        ends_row = (FULL, SUBLANES - HALO)
        target[place, :] = 2.0 * row_of(10, *ends_row) - row_of(0, *ends_row)
        for group in range(FULL * PLANES // GROUP):
            blocks = []
            for number in range(group * GROUP, (group + 1) * GROUP):
                index, extra = divmod(number, FULL)
                blocks.append(row_of(index, extra, SUBLANES - FULL + extra))
            for number, block in enumerate(pack_blocks(blocks)):
                place = at + (group * (GROUP - 1) + number) * SUBLANES
                target[pl.ds(place, SUBLANES), :] = block


def load_inputs(arrays, widths, tiles_count):
    row_count, flat_count = arrays[0].shape
    packet_rows = PAIRS * row_count + END_ROWS
    return pl.pallas_call(
        functools.partial(load_kernel, tiles_count),
        out_shape=[
            pltpu.SMEM((4,), jnp.int32),
            jax.ShapeDtypeStruct((FIELDS, row_count, flat_count), jnp.float32),
            jax.ShapeDtypeStruct((row_count, flat_count), jnp.int32),
            jax.ShapeDtypeStruct((packet_rows, LANES), jnp.float32),
            jax.ShapeDtypeStruct((END_ROWS, LANES), jnp.float32),
        ],
        in_specs=[HBM] * 6,
        out_specs=[SMEM, VMEM, VMEM, VMEM, VMEM],
        scratch_shapes=[
            pltpu.VMEM((PLANES, SUBLANES * SUBLANES, LANES), jnp.float32),
            pltpu.VMEM((PLANES, SUBLANES * SUBLANES, LANES), jnp.float32),
            pltpu.SMEM(widths.shape, jnp.int32),
            pltpu.SemaphoreType.DMA((7,)),
        ],
        compiler_params=pltpu.CompilerParams(vmem_limit_bytes=16 * 1024 * 1024),
        name="load",
    )(*[pltpu.with_memory_space_constraint(array, pltpu.HBM) for array in (*arrays, widths)])


def spread_kernel(raw, raw_solid, spread):
    for index in range(PLANES):
        for row in range(0, raw_solid.shape[0], SUBLANES):
            spread_tile(raw, raw_solid, index, row, spread, row)


def spread_rows(raw, raw_solid):
    row_count = raw_solid.shape[0]
    return pl.pallas_call(
        spread_kernel,
        out_shape=jax.ShapeDtypeStruct((PLANES, row_count * SUBLANES, LANES), jnp.float32),
        in_specs=[VMEM, VMEM],
        out_specs=VMEM,
        compiler_params=pltpu.CompilerParams(vmem_limit_bytes=16 * 1024 * 1024),
        cost_estimate=pl.CostEstimate(flops=1_000_000, bytes_accessed=4_000_000, transcendentals=0),
        name="spread",
    )(raw, raw_solid)


def join_kernel(info, spread, packet, mine, whole, ends):
    low_part = info[3] == 0
    row_count = spread.shape[1] // SUBLANES
    ends[pl.ds(0, END_ROWS), :] = mine[...]
    ends[pl.ds(END_ROWS, END_ROWS), :] = packet[pl.ds(PAIRS * row_count, END_ROWS), :]
    for pair in range(PAIRS):
        for row in range(0, row_count, SUBLANES):
            both = packet[pl.ds(pair * row_count + row, SUBLANES), :]
            start = row * SUBLANES
            for index, values in ((pair, both), (pair + PAIRS, pltpu.roll(both, HALF, 1))):
                below = jnp.where(low_part, 0.0, values)
                above = jnp.where(low_part, values, 0.0)
                whole[index, pl.ds(start, SUBLANES, stride=SUBLANES), :] = below
                whole[index, pl.ds(start + SUBLANES - 1, SUBLANES, stride=SUBLANES), :] = above


def join_parts(info, spread, packet, mine):
    return pl.pallas_call(
        join_kernel,
        out_shape=[
            jax.ShapeDtypeStruct(spread.shape, jnp.float32),
            jax.ShapeDtypeStruct((2 * END_ROWS, LANES), jnp.float32),
        ],
        in_specs=[SMEM, VMEM, VMEM, VMEM],
        out_specs=[VMEM] * 2,
        input_output_aliases={1: 0},
        compiler_params=pltpu.CompilerParams(vmem_limit_bytes=16 * 1024 * 1024),
        name="join",
    )(info, pltpu.with_memory_space_constraint(spread, pltpu.VMEM), packet, mine)


def keep_rows(target, target_index, source, index, rows, size):
    for place, row in enumerate(rows):
        target[target_index, flat_rows(place * size, size), :] = source[
            index, flat_rows(row, size), :
        ]


def collide_rows(geometry, before, whole, first, colours, walls, state):
    over_rows(geometry, first - 1, *COLOUR_BLOCK, lambda block: colour_stage(
        block, geometry, before, colours))
    over_rows(geometry, first, *COLLIDE_BLOCK, lambda block: collide_stage(
        block, geometry, before, whole, colours, walls, state))


def keep_state(target, state, rows):
    place = 0
    for part in state:
        for index in range(part.shape[0]):
            keep_rows(target, place, part, index, rows, KEPT)
            place += 1


def first_kernel(
    info, whole, moved_later, reds_later, crossed_later,
    state_rim, fields_rim, state_later_rim, final_rim,
    colours, walls, moved, reds, crossed, fields,
):
    state, later = (moved, reds, crossed), (moved_later, reds_later, crossed_later)
    geometry = Geometry(info, OWN_TILES)
    live = geometry.live
    fill_wall_table(walls, geometry)
    collide_rows(geometry, whole, whole, 1, colours, walls, state)
    over_rows(geometry, 2, *ARRIVE_BLOCK, lambda block: arrive_stage(
        block, geometry, walls, state, fields))
    keep_state(state_rim, state, (1, live - 3))
    for index in range(FIELDS):
        keep_rows(fields_rim, index, fields, index, (2, live - 4), KEPT)
    collide_rows(geometry, fields, whole, 3, colours, walls, later)
    edge = Block(geometry, [(RIM, RIM, RIM), (live - 2 * RIM, live - 2 * RIM, RIM)], True, [0, RIM])
    arrive_stage(edge, geometry, walls, later, final_rim)
    keep_state(state_later_rim, later, (3, live - 5))


def tile_copies(pieces, outs, held_row, out_row, sems):
    held, rows = pl.ds(held_row, SUBLANES), pl.ds(out_row, SUBLANES)
    parts = (
        (pieces.at[0, held], outs[0].at[rows]),
        (pieces.at[pl.ds(1, 3), held], outs[1].at[:, rows]),
        (pieces.at[pl.ds(4, 6), held], outs[2].at[:, rows]),
        (pieces.at[10, held], outs[3].at[rows]),
    )
    return [
        pltpu.make_async_copy(source, target, sems.at[number])
        for number, (source, target) in enumerate(parts)
    ]


def gather_tiles(final, row, pieces, held_row):
    for index in range(FIELDS):
        for tile in range(OWN_TILES):
            start = pl.multiple_of(row * SUBLANES, SUBLANES) + 1 + tile
            pieces[index, pl.ds(held_row, SUBLANES), pl.ds(tile * LANES, LANES)] = final[
                index, pl.ds(start, SUBLANES, stride=SUBLANES), :
            ]


def second_kernel(
    info, moved, reds, crossed, arrived, density_out, momentum_out, stress_out, red_out,
    final, walls, pieces, zeros, sems,
):
    outs = (density_out, momentum_out, stress_out, red_out)
    row_tiles = density_out.shape[0] // SUBLANES
    geometry = Geometry(info, OWN_TILES)
    live = geometry.live
    fill_wall_table(walls, geometry)

    zeros[...] = jnp.zeros(zeros.shape, zeros.dtype)
    dead = {}
    for tile in range(row_tiles):
        dead[tile] = tile_copies(zeros, outs, 0, tile * SUBLANES, sems.at[tile])

        @pl.when(tile * SUBLANES >= live)
        def _():
            for copy in dead[tile]:
                copy.start()

    def copies_of(tile):
        row = pl.multiple_of(tile * SUBLANES, SUBLANES)
        return tile_copies(pieces, outs, row, row, sems.at[tile])

    def finish(tile, carry):
        row = pl.multiple_of(tile * SUBLANES, SUBLANES)
        block = Block(geometry, [(row, row, SUBLANES)], inner=True)
        arrive_stage(block, geometry, walls, (moved, reds, crossed), final)
        gather_tiles(final, row, pieces, row)
        for copy in copies_of(tile):
            copy.start()
        return carry

    def settle(tile, carry):
        for copy in copies_of(tile):
            copy.wait()
        return carry

    last = live // SUBLANES - 1
    lax.fori_loop(1, last, finish, 0)
    lax.fori_loop(1, last, settle, 0)
    for tile in range(row_tiles):

        @pl.when(tile * SUBLANES >= live)
        def _():
            for copy in dead[tile]:
                copy.wait()


def rim_shape(count, rows):
    return jax.ShapeDtypeStruct((count, rows * SUBLANES, LANES), jnp.float32)


def state_shapes(flat):
    return [jax.ShapeDtypeStruct((count, flat, LANES), jnp.float32) for count in (MOVED, REDS, CROSSED)]


def run_first(info, whole):
    flat = whole.shape[1]
    state_rim = rim_shape(MOVED + REDS + CROSSED, 2 * KEPT)
    shapes = state_shapes(flat)
    shapes = shapes + [state_rim, rim_shape(FIELDS, 2 * KEPT), state_rim, rim_shape(FIELDS, 2 * RIM)]
    return pl.pallas_call(
        first_kernel,
        out_shape=shapes,
        in_specs=[SMEM, VMEM],
        out_specs=[VMEM] * len(shapes),
        scratch_shapes=[
            pltpu.VMEM((4, flat, LANES), jnp.float32),
            pltpu.VMEM((4, 3 * SUBLANES, LANES), jnp.float32),
        ]
        + [pltpu.VMEM(shape.shape, shape.dtype) for shape in state_shapes(flat)]
        + [pltpu.VMEM((FIELDS, flat, LANES), jnp.float32)],
        compiler_params=pltpu.CompilerParams(vmem_limit_bytes=24 * 1024 * 1024),
        cost_estimate=pl.CostEstimate(flops=20_000_000, bytes_accessed=8_000_000, transcendentals=0),
        name="first",
    )(info, whole)


def run_second(info, state, arrived, arrays):
    flat = state[0].shape[1]
    row_count, flat_count = arrays[0].shape
    shapes = [jax.ShapeDtypeStruct(array.shape, jnp.float32) for array in arrays[:4]]
    return pl.pallas_call(
        second_kernel,
        out_shape=shapes,
        in_specs=[SMEM, VMEM, VMEM, VMEM, ANY],
        out_specs=[ANY] * 4,
        scratch_shapes=[
            pltpu.VMEM((FIELDS, flat, LANES), jnp.float32),
            pltpu.VMEM((4, 3 * SUBLANES, LANES), jnp.float32),
            pltpu.VMEM((FIELDS, row_count, flat_count), jnp.float32),
            pltpu.VMEM((FIELDS, SUBLANES, flat_count), jnp.float32),
            pltpu.SemaphoreType.DMA((row_count // SUBLANES, 4)),
        ],
        compiler_params=pltpu.CompilerParams(vmem_limit_bytes=24 * 1024 * 1024),
        cost_estimate=pl.CostEstimate(flops=20_000_000, bytes_accessed=8_000_000, transcendentals=0),
        name="second",
    )(info, *state, arrived)


def follow_kernel(ends, kept, out):
    out[pl.ds(PACKED * SUBLANES, 1), :] = jnp.zeros((1, LANES), jnp.float32)


def follow(ends, kept):
    return pl.pallas_call(
        follow_kernel,
        out_shape=jax.ShapeDtypeStruct(ends.shape, jnp.float32),
        in_specs=[VMEM, ANY],
        out_specs=VMEM,
        input_output_aliases={0: 0},
        compiler_params=pltpu.CompilerParams(vmem_limit_bytes=8 * 1024 * 1024),
        name="follow",
    )(pltpu.with_memory_space_constraint(ends, pltpu.VMEM), kept)


def outer_kernel(
    info, whole, arrived, passed, state_rim, fields_rim, state_later_rim, final_rim, *refs,
):
    outs = refs[4:8]
    start_fields, colours, walls, fields, final = refs[8:13]
    state, later = refs[13:16], refs[16:19]
    pieces, sems = refs[19:]
    geometry = Geometry(info, OWN_TILES)
    live = geometry.live
    low_part = info[3] == 0
    fill_wall_table(walls, geometry)

    def ends_of(ref, half):
        blocks = []
        for group in range(FULL * PLANES // GROUP):
            first = half * (PACKED + 1) + group * (GROUP - 1)
            packed = [ref[pl.ds((first + k) * SUBLANES, SUBLANES), :] for k in range(GROUP - 1)]
            blocks = blocks + unpack_blocks(packed)
        last = half * (PACKED + 1) + PACKED
        return blocks + [ref[pl.ds(last * SUBLANES, SUBLANES), :]]

    tiles = block_tiles()
    middle = (tiles >= 1) & (tiles <= OWN_TILES)

    def widened(own, other):
        beside = jnp.where(tiles == 0, roll_tiles(other, -OWN_TILES), roll_tiles(other, OWN_TILES))
        return jnp.where(geometry.domain, jnp.where(middle, own, beside), 0.0)

    straight = [widened(*pair) for pair in zip(ends_of(arrived, 0), ends_of(arrived, 1))]
    crossed = [widened(*pair) for pair in zip(ends_of(passed, 1), ends_of(passed, 0))]
    below = [jnp.where(low_part, *pair) for pair in zip(straight, crossed)]
    above = [jnp.where(low_part, *pair) for pair in zip(crossed, straight)]

    def spans(first, count):
        mirrored = SLAB - first - count
        return [
            (first - HALO, first, count),
            (live - 2 * RIM + mirrored, SLAB + mirrored, count),
        ]

    for index in range(PLANES):
        for extra in range(FULL):
            number = FULL * index + extra
            start_fields[index, flat_rows(1 + extra, 1), :] = below[number]
            start_fields[index, flat_rows(2 * SLAB - HALO + extra, 1), :] = above[number]
        start_fields[index, flat_rows(HALO, 2), :] = whole[index, flat_rows(0, 2), :]
        start_fields[index, flat_rows(2 * SLAB - HALO - 2, 2), :] = whole[
            index, flat_rows(live - 2, 2), :
        ]
    for row, colour in ((0, below[-1]), (2 * SLAB - 1, above[-1])):
        start_fields[0, flat_rows(row, 1), :] = jnp.zeros((SUBLANES, LANES), jnp.float32)
        start_fields[10, flat_rows(row, 1), :] = 0.5 * colour

    def place(target, index, source, at, first, size):
        for place, (row, local, count) in enumerate(spans(first, size)):
            target[index, flat_rows(local, size), :] = source[at, flat_rows(place * size, size), :]

    for parts, rim, first in ((state, state_rim, HALO + 1), (later, state_later_rim, HALO + 3)):
        at = 0
        for part in parts:
            for index in range(part.shape[0]):
                place(part, index, rim, at, first, KEPT)
                at += 1
    for index in range(FIELDS):
        place(fields, index, fields_rim, index, HALO + 2, 2)
        place(final, index, final_rim, index, HALO + RIM, RIM)

    block = lambda first, count: Block(geometry, spans(first, count))
    colour_stage(block(0, 6), geometry, start_fields, colours)
    collide_stage(block(1, 4), geometry, start_fields, start_fields, colours, walls, state)
    arrive_stage(block(2, 4), geometry, walls, state, fields)
    start_fields[PLANES - 1, flat_rows(HALO + 2, 1), :] = whole[PLANES - 1, flat_rows(2, 1), :]
    start_fields[PLANES - 1, flat_rows(2 * SLAB - HALO - 3, 1), :] = whole[
        PLANES - 1, flat_rows(live - 3, 1), :
    ]
    colour_stage(block(2, 6), geometry, fields, colours)
    collide_stage(block(3, 4), geometry, fields, start_fields, colours, walls, later)
    arrive_stage(block(4, 4), geometry, walls, later, final)

    copies = []
    for side, row, out_row in ((0, HALO, 0), (1, SLAB, live - SUBLANES)):
        gather_tiles(final, row, pieces, side * SUBLANES)
        out_row = pl.multiple_of(out_row, SUBLANES)
        copies = copies + tile_copies(pieces, outs, side * SUBLANES, out_row, sems.at[side])
    for copy in copies:
        copy.start()
    for copy in copies:
        copy.wait()


def run_outer(info, whole, arrived, passed, rims, outs):
    flat = 2 * SLAB * SUBLANES
    flat_count = outs[0].shape[1]
    return pl.pallas_call(
        outer_kernel,
        out_shape=[jax.ShapeDtypeStruct(out.shape, jnp.float32) for out in outs],
        in_specs=[SMEM] + [VMEM] * 7 + [ANY] * 4,
        out_specs=[ANY] * 4,
        scratch_shapes=[
            pltpu.VMEM((PLANES, flat, LANES), jnp.float32),
            pltpu.VMEM((4, flat, LANES), jnp.float32),
            pltpu.VMEM((4, 3 * SUBLANES, LANES), jnp.float32),
            pltpu.VMEM((FIELDS, flat, LANES), jnp.float32),
            pltpu.VMEM((FIELDS, flat, LANES), jnp.float32),
        ]
        + [pltpu.VMEM(shape.shape, shape.dtype) for shape in 2 * state_shapes(flat)]
        + [
            pltpu.VMEM((FIELDS, 2 * SUBLANES, flat_count), jnp.float32),
            pltpu.SemaphoreType.DMA((2, 4)),
        ],
        input_output_aliases={8: 0, 9: 1, 10: 2, 11: 3},
        compiler_params=pltpu.CompilerParams(vmem_limit_bytes=32 * 1024 * 1024),
        name="outer",
    )(info, whole, arrived, passed, *rims, *outs)


def body(density, momentum, stress, red_density, solid, widths):
    tiles_count = lax.axis_size("tiles")
    arrays = (density, momentum, stress, red_density, solid)
    info, raw, raw_solid, packet, mine = load_inputs(arrays, widths, tiles_count)
    info = pltpu.with_memory_space_constraint(info, pltpu.SMEM)
    swap = [(0, 1), (1, 0)]
    packet = lax.ppermute(packet, "sub", swap)
    spread = spread_rows(raw, raw_solid)
    whole, ends = join_parts(info, spread, packet, mine)
    route = [(2 * k, 2 * k + 2) for k in range(tiles_count - 1)]
    route = route + [(2 * k + 3, 2 * k + 1) for k in range(tiles_count - 1)]
    arrived = lax.ppermute(ends, ("tiles", "sub"), route)
    *state, state_rim, fields_rim, state_later_rim, final_rim = run_first(info, whole)
    arrived = follow(arrived, fields_rim)
    passed = lax.ppermute(arrived, "sub", swap)
    outs = run_second(info, state, arrived, arrays)
    rims = (state_rim, fields_rim, state_later_rim, final_rim)
    return tuple(run_outer(info, whole, arrived, passed, rims, outs))


def solution(mesh):
    in_specs = (
        P(("groups", "tiles"), "sub"),
        P(None, ("groups", "tiles"), "sub"),
        P(None, ("groups", "tiles"), "sub"),
        P(("groups", "tiles"), "sub"),
        P(("groups", "tiles"), "sub"),
        P("groups"),
    )
    out_specs = (
        P(("groups", "tiles"), "sub"),
        P(None, ("groups", "tiles"), "sub"),
        P(None, ("groups", "tiles"), "sub"),
        P(("groups", "tiles"), "sub"),
    )
    return jax.shard_map(body, mesh=mesh, in_specs=in_specs, out_specs=out_specs, check_vma=False)
```

profile of v0, /device:TPU:5, one launch (start us, length us, event | category | flops | bytes accessed | tf_op | source)
XLA Modules:
  0.0 20.0 jit_solution(10853224039854890659)
XLA Ops:
  0.6 1.6 %load.1 = (s32[4]{0:T(128)S(4)}, f32[11,48,768]{2,1,0:T(8,128)S(1)}, s32[48,768]{1,0:T(8,128)S(1)}, f32[512,128]{1,0:T(8,128)S(1)}, f32[224,128]{1,0:T(8,128)S(1)}) custom-call(f32[48,768]{1,0:T(8,128)} %density.1, f32[3,48,768]{2,1,0:T(8,128)} %momentum.1, f32[6,48,768]{2,1,0:T(8,128)} %stress.1, f32[48,768]{1,0:T(8,128)} %red.1, s32[48,768]{1,0:T(8,128)} %solid.1, ...), custom_call_target="tpu_custom_call" | custom-call | tf_op jit(solution)/shard_map/load/pallas_call | solution.py:526
  2.3 0.7 %collective-permute-start = (f32[512,128]{1,0:T(8,128)S(1)}, f32[512,128]{1,0:T(8,128)S(1)}, u32[]{:S(2)}, u32[]{:S(2)}) collective-permute-start(f32[512,128]{1,0:T(8,128)S(1)} %get-tuple-element.25), channel_id=1, source_target_pairs={{0,1},{1,0},{2,3},{3,2},{4,5},{5,4},{6,7},{7,6},{8,9},{9,8},{10,11... | collective-permute-start | bytes 786440 | tf_op jit(solution)/shard_map/ppermute | solution.py:903
  3.0 0.3 %spread.1 = f32[12,384,128]{2,1,0:T(8,128)S(1)} custom-call(f32[11,48,768]{2,1,0:T(8,128)S(1)} %get-tuple-element.23.raw, s32[48,768]{1,0:T(8,128)S(1)} %get-tuple-element.24.raw_solid), custom_call_target="tpu_custom_call" | custom-call | flops 1000000 | bytes 4000000 | tf_op jit(solution)/shard_map/spread/pallas_call | solution.py:556
  3.3 0.9 %collective-permute-done.packet = f32[512,128]{1,0:T(8,128)S(1)} collective-permute-done((f32[512,128]{1,0:T(8,128)S(1)}, f32[512,128]{1,0:T(8,128)S(1)}, u32[]{:S(2)}, u32[]{:S(2)}) %collective-permute-start) | collective-permute-done | bytes 262176 | tf_op jit(solution)/shard_map/ppermute | solution.py:903
  4.2 0.1 join.1
  4.3 1.9 %collective-permute-start.1 = (f32[448,128]{1,0:T(8,128)S(1)}, f32[448,128]{1,0:T(8,128)S(1)}, u32[]{:S(2)}, u32[]{:S(2)}) collective-permute-start(f32[448,128]{1,0:T(8,128)S(1)} %get-tuple-element.28), channel_id=1, source_target_pairs={{0,2},{2,4},{4,6},{6,8},{8,10},{10,12},{12,14},{3,1},{5,3},{7,5},{... | collective-permute-start | bytes 688136 | tf_op jit(solution)/shard_map/ppermute | solution.py:908
  6.2 7.0 %first.1 = (f32[19,384,128]{2,1,0:T(8,128)S(1)}, f32[5,384,128]{2,1,0:T(8,128)S(1)}, f32[10,384,128]{2,1,0:T(8,128)S(1)}, f32[34,32,128]{2,1,0:T(8,128)S(1)}, f3...) custom-call(s32[4]{0:T(128)S(4)} %get-tuple-element.22.info, ...), custom_call_target="tpu_custom_call" | custom-call | flops 20000000 | bytes 8000000 | tf_op jit(solution)/shard_map/first/pallas_call | solution.py:726
  13.2 0.0 collective-permute-done.1.ends
  13.2 1.9 %collective-permute-start.2 = (f32[448,128]{1,0:T(8,128)S(1)}, f32[448,128]{1,0:T(8,128)S(1)}, u32[]{:S(2)}, u32[]{:S(2)}) collective-permute-start(f32[448,128]{1,0:T(8,128)S(1)} %follow.1.arrived), channel_id=1, source_target_pairs={{0,1},{1,0},{2,3},{3,2},{4,5},{5,4},{6,7},{7,6},{8,9},{9,8},{10,11... | collective-permute-start | bytes 688136 | tf_op jit(solution)/shard_map/ppermute | solution.py:911
  15.2 2.5 %second.1 = (f32[48,768]{1,0:T(8,128)}, f32[3,48,768]{2,1,0:T(8,128)}, f32[6,48,768]{2,1,0:T(8,128)}, f32[48,768]{1,0:T(8,128)}) custom-call(s32[4]{0:T(128)S(4)} %get-tuple-element.22.info, f32[19,384,128]{2,1,0:T(8,128)S(1)} %get-tuple-element.33.moved, f32[5,384,128]{2,1,0:T(8,128)S(1)} %get-tuple-element.34.reds, ...), custom_call_target="tpu_custom_call" | custom-call | flops 20000000 | bytes 8000000 | tf_op jit(solution)/shard_map/second/pallas_call | solution.py:747
  17.7 0.0 collective-permute-done.2.passed
  17.7 2.3 %outer.1 = (f32[48,768]{1,0:T(8,128)}, f32[3,48,768]{2,1,0:T(8,128)}, f32[6,48,768]{2,1,0:T(8,128)}, f32[48,768]{1,0:T(8,128)}) custom-call(s32[4]{0:T(128)S(4)} %get-tuple-element.22.info, f32[12,384,128]{2,1,0:T(8,128)S(1)} %get-tuple-element.27.whole, ...), custom_call_target="tpu_custom_call", output_to_operand_aliasing={{0}: (8, {}), {1}: (9, {}), {2}: (10, {}), {3}: (11, {})} | custom-call | tf_op jit(solution)/shard_map/outer/pallas_call | solution.py:874
  (1 shorter events, 0.0 us)
Async XLA Ops:
  2.3 1.9 %collective-permute-start = (f32[512,128]{1,0:T(8,128)S(1)}, f32[512,128]{1,0:T(8,128)S(1)}, u32[]{:S(2)}, u32[]{:S(2)}) collective-permute-start(f32[512,128]{1,0:T(8,128)S(1)} %get-tuple-element.25), channel_id=1, source_target_pairs={{0,1},{1,0},{2,3},{3,2},{4,5},{5,4},{6,7},{7,6},{8,9},{9,8},{10,11... | collective-permute-start | bytes 786440 | tf_op jit(solution)/shard_map/ppermute | solution.py:903
  4.3 8.9 %collective-permute-start.1 = (f32[448,128]{1,0:T(8,128)S(1)}, f32[448,128]{1,0:T(8,128)S(1)}, u32[]{:S(2)}, u32[]{:S(2)}) collective-permute-start(f32[448,128]{1,0:T(8,128)S(1)} %get-tuple-element.28), channel_id=1, source_target_pairs={{0,2},{2,4},{4,6},{6,8},{8,10},{10,12},{12,14},{3,1},{5,3},{7,5},{... | collective-permute-start | bytes 688136 | tf_op jit(solution)/shard_map/ppermute | solution.py:908
  13.2 4.4 %collective-permute-start.2 = (f32[448,128]{1,0:T(8,128)S(1)}, f32[448,128]{1,0:T(8,128)S(1)}, u32[]{:S(2)}, u32[]{:S(2)}) collective-permute-start(f32[448,128]{1,0:T(8,128)S(1)} %follow.1.arrived), channel_id=1, source_target_pairs={{0,1},{1,0},{2,3},{3,2},{4,5},{5,4},{6,7},{7,6},{8,9},{9,8},{10,11... | collective-permute-start | bytes 688136 | tf_op jit(solution)/shard_map/ppermute | solution.py:911
where the time goes:
time: 20.1 us; the launch traced here: 20 us
  Pallas kernels  13.8 us (69%)
  starting transfers between devices  4.61 us (23%)
  waiting for transfers between devices  0.86 us (4%)
  between operations  0.7 us (3%)
    pallas_call x1, Pallas kernels, run_first(): pl.pallas_call(first_kernel, out_shape=shapes, in_specs=[SMEM, VMEM], out...  6.97 us
    pallas_call x1, Pallas kernels, run_second(): pl.pallas_call(second_kernel, out_shape=shapes, in_specs=[SMEM, VMEM, VME...  2.46 us
    pallas_call x1, Pallas kernels, run_outer(): pl.pallas_call(outer_kernel, out_shape=[jax.ShapeDtypeStruct(out.shape, j...  2.29 us
    ppermute x1, starting transfers between devices, body(): passed = lax.ppermute(arrived, 'sub', swap)  1.95 us
    ppermute x1, starting transfers between devices, body(): arrived = lax.ppermute(ends, ('tiles', 'sub'), route)  1.92 us
    pallas_call x1, Pallas kernels, load_inputs(): pl.pallas_call(functools.partial(load_kernel, tiles_count), out_shape=[pl...  1.65 us
    ppermute x1, waiting for transfers between devices, body(): packet = lax.ppermute(packet, 'sub', swap)  0.86 us
    ppermute x1, starting transfers between devices, body(): packet = lax.ppermute(packet, 'sub', swap)  0.74 us
  transfers between devices with their start and end apart: 3, of which 1 were waited for; matrix products, arithmetic and copies ran while one was open for 0% of the time, Pallas kernels for 49%

commit v1 on v0

--- a/solution.py
+++ b/solution.py
@@ -21,6 +21,7 @@
 PLANES = FIELDS + 1
 MOVED = 19
 REDS = 5
+HELD = MOVED + 1
 RIM = 4
 SLAB = HALO + 2 * RIM
 OWN_TILES = SUBLANES - 2
@@ -134,6 +135,27 @@
     return pl.ds(start + tile_offset, count * SUBLANES)
 
 
+class ByRow:
+    def __init__(self, ref):
+        self.ref = ref
+
+
+def place_of(ref, index, row, tile_offset=0):
+    if isinstance(ref, ByRow):
+        return ref.ref, row, pl.ds(index * SUBLANES + tile_offset, SUBLANES)
+    return ref, index, flat_rows(row, 1, tile_offset)
+
+
+def read_row(ref, index, row, tile_offset=0):
+    ref, first, second = place_of(ref, index, row, tile_offset)
+    return ref[first, second, :]
+
+
+def write_row(ref, index, row, values):
+    ref, first, second = place_of(ref, index, row)
+    ref[first, second, :] = values
+
+
 class Block:
     def __init__(self, geometry, spans, inner=False, store_rows=None):
         self.spans = spans
@@ -156,9 +178,9 @@
             for row in rows
         ]
 
-    def load(self, ref, index, offset=0):
+    def load(self, ref, index, offset=0, tile_offset=0):
         return Rows([
-            ref[index, flat_rows(local + offset + extra, 1), :]
+            read_row(ref, index, local + offset + extra, tile_offset)
             for row, local, count in self.spans
             for extra in range(count)
         ])
@@ -170,14 +192,7 @@
             for extra in range(count)
         ]
         for target, part in zip(targets, values.parts):
-            ref[index, flat_rows(target, 1), :] = part
-
-    def store_crossed(self, geometry, ref, index, vel_y, values):
-        mask = geometry.last_lanes if vel_y == 1 else geometry.first_lanes
-        rows = [local + extra for row, local, count in self.spans for extra in range(count)]
-        for row, part in zip(rows, values.parts):
-            ref[index, flat_rows(row, 1), :] = part
-            pltpu.store(ref.at[index, flat_rows(row, 1, vel_y), :], part, mask=mask)
+            write_row(ref, index, target, part)
 
     def wall_terms(self, walls, position):
         terms = [walls[position, flat_rows(kind, 1), :] for kind in self.kinds]
@@ -212,8 +227,6 @@
     for one, two in ((1, 1), (-1, -1), (1, -1), (-1, 1))
 )
 VELOCITIES = ((0, 0, 0),) + VELOCITIES
-SIDEWAYS = tuple(place for place, velocity in enumerate(VELOCITIES) if velocity[1] != 0)
-CROSSED = len(SIDEWAYS)
 
 
 def colour_stage(block, geometry, fields, colours):
@@ -271,30 +284,23 @@
     run = [sign * part for part in flux]
     mixing = ((SEPARATION / 144.0) * red) * ((density - red) * inverse)
     red_run = [0.5 * part + mixing * grad for part, grad in zip(run, grads)]
-    moved, reds, crossed = state
-
-    def leave(direction, values):
-        block.store(moved, direction, values)
-        if direction in SIDEWAYS:
-            place = SIDEWAYS.index(direction)
-            block.store_crossed(geometry, crossed, place, VELOCITIES[direction][1], values)
-
-    leave(0, 12.0 * base)
+    moved, reds = state
+    block.store(moved, 0, 12.0 * base)
     straight = [base + part for part in own]
     for axis in range(3):
         middle = 2.0 * straight[axis]
         swing = 2.0 * run[axis]
-        leave(1 + 2 * axis, middle + swing)
-        leave(2 + 2 * axis, middle - swing)
+        block.store(moved, 1 + 2 * axis, middle + swing)
+        block.store(moved, 2 + 2 * axis, middle - swing)
     for plane, (a, b) in enumerate(((0, 1), (0, 2), (1, 2))):
         middle = straight[a] + own[b]
         same, other = middle + cross[plane], middle - cross[plane]
         along, against = run[a] + run[b], run[a] - run[b]
         first = 7 + 4 * plane
-        leave(first, same + along)
-        leave(first + 1, same - along)
-        leave(first + 2, other + against)
-        leave(first + 3, other - against)
+        block.store(moved, first, same + along)
+        block.store(moved, first + 1, same - along)
+        block.store(moved, first + 2, other + against)
+        block.store(moved, first + 3, other - against)
 
     red_base = select(block.valid, red * (1.0 / 36.0), 0.0)
     red_run = [select(block.valid, part, 0.0) for part in red_run]
@@ -307,7 +313,7 @@
 
 def arrive_stage(block, geometry, walls, state, fields):
     third = 1.0 / 3.0
-    moved, reds, crossed = state
+    moved, reds = state
     own = [None] * MOVED
 
     def here(direction):
@@ -317,10 +323,11 @@
 
     def arrived(direction, opposite):
         vel_x, vel_y, vel_z = VELOCITIES[direction]
+        values = here(direction) if vel_x == 0 else block.load(moved, direction, -vel_x)
         if vel_y != 0:
-            values = block.load(crossed, SIDEWAYS.index(direction), -vel_x)
-        else:
-            values = here(direction) if vel_x == 0 else block.load(moved, direction, -vel_x)
+            beside = block.load(moved, direction, -vel_x, -vel_y)
+            leaving = geometry.last_lanes if vel_y == 1 else geometry.first_lanes
+            values = select(leaving, beside, values)
         if vel_y != 0 or vel_z != 0:
             values = roll_lanes(values, TILE * vel_y + vel_z)
         masks = []
@@ -595,11 +602,10 @@
     )(info, pltpu.with_memory_space_constraint(spread, pltpu.VMEM), packet, mine)
 
 
-def keep_rows(target, target_index, source, index, rows, size):
+def keep_rows(target, source, rows, size):
     for place, row in enumerate(rows):
-        target[target_index, flat_rows(place * size, size), :] = source[
-            index, flat_rows(row, size), :
-        ]
+        for extra in range(size):
+            target[place * size + extra] = source[row + extra]
 
 
 def collide_rows(geometry, before, whole, first, colours, walls, state):
@@ -609,33 +615,26 @@
         block, geometry, before, whole, colours, walls, state))
 
 
-def keep_state(target, state, rows):
-    place = 0
-    for part in state:
-        for index in range(part.shape[0]):
-            keep_rows(target, place, part, index, rows, KEPT)
-            place += 1
-
-
 def first_kernel(
-    info, whole, moved_later, reds_later, crossed_later,
-    state_rim, fields_rim, state_later_rim, final_rim,
-    colours, walls, moved, reds, crossed, fields,
+    info, whole, moved_later, reds_later,
+    moved_rim, reds_rim, fields_rim, moved_later_rim, reds_later_rim, final_rim,
+    colours, walls, moved, reds, fields,
 ):
-    state, later = (moved, reds, crossed), (moved_later, reds_later, crossed_later)
+    state, later = (ByRow(moved), ByRow(reds)), (ByRow(moved_later), ByRow(reds_later))
     geometry = Geometry(info, OWN_TILES)
     live = geometry.live
     fill_wall_table(walls, geometry)
-    collide_rows(geometry, whole, whole, 1, colours, walls, state)
+    collide_rows(geometry, whole, whole, 1, ByRow(colours), walls, state)
     over_rows(geometry, 2, *ARRIVE_BLOCK, lambda block: arrive_stage(
-        block, geometry, walls, state, fields))
-    keep_state(state_rim, state, (1, live - 3))
-    for index in range(FIELDS):
-        keep_rows(fields_rim, index, fields, index, (2, live - 4), KEPT)
-    collide_rows(geometry, fields, whole, 3, colours, walls, later)
+        block, geometry, walls, state, ByRow(fields)))
+    keep_rows(moved_rim, moved, (1, live - 3), KEPT)
+    keep_rows(reds_rim, reds, (1, live - 3), KEPT)
+    keep_rows(fields_rim, fields, (2, live - 4), KEPT)
+    collide_rows(geometry, ByRow(fields), whole, 3, ByRow(colours), walls, later)
     edge = Block(geometry, [(RIM, RIM, RIM), (live - 2 * RIM, live - 2 * RIM, RIM)], True, [0, RIM])
     arrive_stage(edge, geometry, walls, later, final_rim)
-    keep_state(state_later_rim, later, (3, live - 5))
+    keep_rows(moved_later_rim, moved_later, (3, live - 5), KEPT)
+    keep_rows(reds_later_rim, reds_later, (3, live - 5), KEPT)
 
 
 def tile_copies(pieces, outs, held_row, out_row, sems):
@@ -662,7 +661,7 @@
 
 
 def second_kernel(
-    info, moved, reds, crossed, arrived, density_out, momentum_out, stress_out, red_out,
+    info, moved, reds, arrived, density_out, momentum_out, stress_out, red_out,
     final, walls, pieces, zeros, sems,
 ):
     outs = (density_out, momentum_out, stress_out, red_out)
@@ -688,7 +687,7 @@
     def finish(tile, carry):
         row = pl.multiple_of(tile * SUBLANES, SUBLANES)
         block = Block(geometry, [(row, row, SUBLANES)], inner=True)
-        arrive_stage(block, geometry, walls, (moved, reds, crossed), final)
+        arrive_stage(block, geometry, walls, (ByRow(moved), ByRow(reds)), final)
         gather_tiles(final, row, pieces, row)
         for copy in copies_of(tile):
             copy.start()
@@ -710,30 +709,29 @@
                 copy.wait()
 
 
-def rim_shape(count, rows):
-    return jax.ShapeDtypeStruct((count, rows * SUBLANES, LANES), jnp.float32)
-
-
-def state_shapes(flat):
-    return [jax.ShapeDtypeStruct((count, flat, LANES), jnp.float32) for count in (MOVED, REDS, CROSSED)]
+def by_row(rows, count):
+    return jax.ShapeDtypeStruct((rows, count * SUBLANES, LANES), jnp.float32)
 
 
 def run_first(info, whole):
-    flat = whole.shape[1]
-    state_rim = rim_shape(MOVED + REDS + CROSSED, 2 * KEPT)
-    shapes = state_shapes(flat)
-    shapes = shapes + [state_rim, rim_shape(FIELDS, 2 * KEPT), state_rim, rim_shape(FIELDS, 2 * RIM)]
+    rows = whole.shape[1] // SUBLANES
+    shapes = [
+        by_row(rows, HELD),
+        by_row(rows, REDS),
+        by_row(2 * KEPT, HELD),
+        by_row(2 * KEPT, REDS),
+        by_row(2 * KEPT, FIELDS),
+        by_row(2 * KEPT, HELD),
+        by_row(2 * KEPT, REDS),
+        jax.ShapeDtypeStruct((FIELDS, 2 * RIM * SUBLANES, LANES), jnp.float32),
+    ]
+    scratch = [by_row(rows, 4), by_row(4, 3), by_row(rows, HELD), by_row(rows, REDS), by_row(rows, FIELDS)]
     return pl.pallas_call(
         first_kernel,
         out_shape=shapes,
         in_specs=[SMEM, VMEM],
         out_specs=[VMEM] * len(shapes),
-        scratch_shapes=[
-            pltpu.VMEM((4, flat, LANES), jnp.float32),
-            pltpu.VMEM((4, 3 * SUBLANES, LANES), jnp.float32),
-        ]
-        + [pltpu.VMEM(shape.shape, shape.dtype) for shape in state_shapes(flat)]
-        + [pltpu.VMEM((FIELDS, flat, LANES), jnp.float32)],
+        scratch_shapes=[pltpu.VMEM(shape.shape, shape.dtype) for shape in scratch],
         compiler_params=pltpu.CompilerParams(vmem_limit_bytes=24 * 1024 * 1024),
         cost_estimate=pl.CostEstimate(flops=20_000_000, bytes_accessed=8_000_000, transcendentals=0),
         name="first",
@@ -741,13 +739,13 @@
 
 
 def run_second(info, state, arrived, arrays):
-    flat = state[0].shape[1]
     row_count, flat_count = arrays[0].shape
+    flat = row_count * SUBLANES
     shapes = [jax.ShapeDtypeStruct(array.shape, jnp.float32) for array in arrays[:4]]
     return pl.pallas_call(
         second_kernel,
         out_shape=shapes,
-        in_specs=[SMEM, VMEM, VMEM, VMEM, ANY],
+        in_specs=[SMEM, VMEM, VMEM, ANY],
         out_specs=[ANY] * 4,
         scratch_shapes=[
             pltpu.VMEM((FIELDS, flat, LANES), jnp.float32),
@@ -779,12 +777,13 @@
 
 
 def outer_kernel(
-    info, whole, arrived, passed, state_rim, fields_rim, state_later_rim, final_rim, *refs,
+    info, whole, arrived, passed,
+    moved_rim, reds_rim, fields_rim, moved_later_rim, reds_later_rim, final_rim, *refs,
 ):
     outs = refs[4:8]
     start_fields, colours, walls, fields, final = refs[8:13]
-    state, later = refs[13:16], refs[16:19]
-    pieces, sems = refs[19:]
+    moved, reds, moved_later, reds_later, pieces, sems = refs[13:]
+    state, later = (ByRow(moved), ByRow(reds)), (ByRow(moved_later), ByRow(reds_later))
     geometry = Geometry(info, OWN_TILES)
     live = geometry.live
     low_part = info[3] == 0
@@ -831,30 +830,30 @@
         start_fields[0, flat_rows(row, 1), :] = jnp.zeros((SUBLANES, LANES), jnp.float32)
         start_fields[10, flat_rows(row, 1), :] = 0.5 * colour
 
-    def place(target, index, source, at, first, size):
-        for place, (row, local, count) in enumerate(spans(first, size)):
-            target[index, flat_rows(local, size), :] = source[at, flat_rows(place * size, size), :]
-
-    for parts, rim, first in ((state, state_rim, HALO + 1), (later, state_later_rim, HALO + 3)):
-        at = 0
-        for part in parts:
-            for index in range(part.shape[0]):
-                place(part, index, rim, at, first, KEPT)
-                at += 1
+    def place(target, source, first, size):
+        for number, (row, local, count) in enumerate(spans(first, size)):
+            for extra in range(size):
+                target[local + extra] = source[number * size + extra]
+
+    place(moved, moved_rim, HALO + 1, KEPT)
+    place(reds, reds_rim, HALO + 1, KEPT)
+    place(fields, fields_rim, HALO + 2, KEPT)
+    place(moved_later, moved_later_rim, HALO + 3, KEPT)
+    place(reds_later, reds_later_rim, HALO + 3, KEPT)
     for index in range(FIELDS):
-        place(fields, index, fields_rim, index, HALO + 2, 2)
-        place(final, index, final_rim, index, HALO + RIM, RIM)
+        for number, (row, local, count) in enumerate(spans(HALO + RIM, RIM)):
+            final[index, flat_rows(local, RIM), :] = final_rim[index, flat_rows(number * RIM, RIM), :]
 
     block = lambda first, count: Block(geometry, spans(first, count))
-    colour_stage(block(0, 6), geometry, start_fields, colours)
-    collide_stage(block(1, 4), geometry, start_fields, start_fields, colours, walls, state)
-    arrive_stage(block(2, 4), geometry, walls, state, fields)
+    colour_stage(block(0, 6), geometry, start_fields, ByRow(colours))
+    collide_stage(block(1, 4), geometry, start_fields, start_fields, ByRow(colours), walls, state)
+    arrive_stage(block(2, 4), geometry, walls, state, ByRow(fields))
     start_fields[PLANES - 1, flat_rows(HALO + 2, 1), :] = whole[PLANES - 1, flat_rows(2, 1), :]
     start_fields[PLANES - 1, flat_rows(2 * SLAB - HALO - 3, 1), :] = whole[
         PLANES - 1, flat_rows(live - 3, 1), :
     ]
-    colour_stage(block(2, 6), geometry, fields, colours)
-    collide_stage(block(3, 4), geometry, fields, start_fields, colours, walls, later)
+    colour_stage(block(2, 6), geometry, ByRow(fields), ByRow(colours))
+    collide_stage(block(3, 4), geometry, ByRow(fields), start_fields, ByRow(colours), walls, later)
     arrive_stage(block(4, 4), geometry, walls, later, final)
 
     copies = []
@@ -870,25 +869,26 @@
 
 def run_outer(info, whole, arrived, passed, rims, outs):
     flat = 2 * SLAB * SUBLANES
+    scratch = lambda count: pltpu.VMEM((2 * SLAB, count * SUBLANES, LANES), jnp.float32)
     flat_count = outs[0].shape[1]
     return pl.pallas_call(
         outer_kernel,
         out_shape=[jax.ShapeDtypeStruct(out.shape, jnp.float32) for out in outs],
-        in_specs=[SMEM] + [VMEM] * 7 + [ANY] * 4,
+        in_specs=[SMEM] + [VMEM] * 9 + [ANY] * 4,
         out_specs=[ANY] * 4,
         scratch_shapes=[
             pltpu.VMEM((PLANES, flat, LANES), jnp.float32),
-            pltpu.VMEM((4, flat, LANES), jnp.float32),
+            scratch(4),
             pltpu.VMEM((4, 3 * SUBLANES, LANES), jnp.float32),
-            pltpu.VMEM((FIELDS, flat, LANES), jnp.float32),
+            scratch(FIELDS),
             pltpu.VMEM((FIELDS, flat, LANES), jnp.float32),
         ]
-        + [pltpu.VMEM(shape.shape, shape.dtype) for shape in 2 * state_shapes(flat)]
+        + [scratch(count) for count in (HELD, REDS, HELD, REDS)]
         + [
             pltpu.VMEM((FIELDS, 2 * SUBLANES, flat_count), jnp.float32),
             pltpu.SemaphoreType.DMA((2, 4)),
         ],
-        input_output_aliases={8: 0, 9: 1, 10: 2, 11: 3},
+        input_output_aliases={10: 0, 11: 1, 12: 2, 13: 3},
         compiler_params=pltpu.CompilerParams(vmem_limit_bytes=32 * 1024 * 1024),
         name="outer",
     )(info, whole, arrived, passed, *rims, *outs)
@@ -906,11 +906,10 @@
     route = [(2 * k, 2 * k + 2) for k in range(tiles_count - 1)]
     route = route + [(2 * k + 3, 2 * k + 1) for k in range(tiles_count - 1)]
     arrived = lax.ppermute(ends, ("tiles", "sub"), route)
-    *state, state_rim, fields_rim, state_later_rim, final_rim = run_first(info, whole)
-    arrived = follow(arrived, fields_rim)
+    moved, reds, *rims = run_first(info, whole)
+    arrived = follow(arrived, rims[-1])
     passed = lax.ppermute(arrived, "sub", swap)
-    outs = run_second(info, state, arrived, arrays)
-    rims = (state_rim, fields_rim, state_later_rim, final_rim)
+    outs = run_second(info, (moved, reds), arrived, arrays)
     return tuple(run_outer(info, whole, arrived, passed, rims, outs))
 
 

time: 20.1 us -> 20 us (level)
  the two profiles are of different devices: /device:TPU:5 before, /device:TPU:13 now
where the time goes in v1:
time: 20 us; the launch traced here: 19.8 us
  Pallas kernels  12.8 us (64%)
  starting transfers between devices  5.44 us (27%)
  waiting for transfers between devices  0.86 us (4%)
  between operations  0.7 us (4%)
    pallas_call x1, Pallas kernels, run_first(): pl.pallas_call(first_kernel, out_shape=shapes, in_specs=[SMEM, VMEM], out...  6.01 us
    ppermute x1, starting transfers between devices, body(): passed = lax.ppermute(arrived, 'sub', swap)  2.57 us
    pallas_call x1, Pallas kernels, run_second(): pl.pallas_call(second_kernel, out_shape=shapes, in_specs=[SMEM, VMEM, VME...  2.46 us
    pallas_call x1, Pallas kernels, run_outer(): pl.pallas_call(outer_kernel, out_shape=[jax.ShapeDtypeStruct(out.shape, j...  2.28 us
    ppermute x1, starting transfers between devices, body(): arrived = lax.ppermute(ends, ('tiles', 'sub'), route)  2.13 us
    pallas_call x1, Pallas kernels, load_inputs(): pl.pallas_call(functools.partial(load_kernel, tiles_count), out_shape=[pl...  1.65 us
    ppermute x1, waiting for transfers between devices, body(): packet = lax.ppermute(packet, 'sub', swap)  0.86 us
    ppermute x1, starting transfers between devices, body(): packet = lax.ppermute(packet, 'sub', swap)  0.74 us
  transfers between devices with their start and end apart: 3, of which 1 were waited for; matrix products, arithmetic and copies ran while one was open for 0% of the time, Pallas kernels for 44%

profile of v1, /device:TPU:13, one launch (start us, length us, event | category | flops | bytes accessed | tf_op | source)
XLA Modules:
  0.0 19.8 jit_solution(7666201348124261828)
XLA Ops:
  0.6 1.6 %load.1 = (s32[4]{0:T(128)S(4)}, f32[11,48,768]{2,1,0:T(8,128)S(1)}, s32[48,768]{1,0:T(8,128)S(1)}, f32[512,128]{1,0:T(8,128)S(1)}, f32[224,128]{1,0:T(8,128)S(1)}) custom-call(f32[48,768]{1,0:T(8,128)} %density.1, f32[3,48,768]{2,1,0:T(8,128)} %momentum.1, f32[6,48,768]{2,1,0:T(8,128)} %stress.1, f32[48,768]{1,0:T(8,128)} %red.1, s32[48,768]{1,0:T(8,128)} %solid.1, ...), custom_call_target="tpu_custom_call" | custom-call | tf_op jit(solution)/shard_map/load/pallas_call | solution.py:533
  2.3 0.7 %collective-permute-start = (f32[512,128]{1,0:T(8,128)S(1)}, f32[512,128]{1,0:T(8,128)S(1)}, u32[]{:S(2)}, u32[]{:S(2)}) collective-permute-start(f32[512,128]{1,0:T(8,128)S(1)} %get-tuple-element.26), channel_id=1, source_target_pairs={{0,1},{1,0},{2,3},{3,2},{4,5},{5,4},{6,7},{7,6},{8,9},{9,8},{10,11... | collective-permute-start | bytes 786440 | tf_op jit(solution)/shard_map/ppermute | solution.py:903
  3.0 0.3 %spread.1 = f32[12,384,128]{2,1,0:T(8,128)S(1)} custom-call(f32[11,48,768]{2,1,0:T(8,128)S(1)} %get-tuple-element.24.raw, s32[48,768]{1,0:T(8,128)S(1)} %get-tuple-element.25.raw_solid), custom_call_target="tpu_custom_call" | custom-call | flops 1000000 | bytes 4000000 | tf_op jit(solution)/shard_map/spread/pallas_call | solution.py:563
  3.3 0.9 %collective-permute-done.packet = f32[512,128]{1,0:T(8,128)S(1)} collective-permute-done((f32[512,128]{1,0:T(8,128)S(1)}, f32[512,128]{1,0:T(8,128)S(1)}, u32[]{:S(2)}, u32[]{:S(2)}) %collective-permute-start) | collective-permute-done | bytes 262176 | tf_op jit(solution)/shard_map/ppermute | solution.py:903
  4.2 0.1 join.1
  4.3 2.1 %collective-permute-start.1 = (f32[448,128]{1,0:T(8,128)S(1)}, f32[448,128]{1,0:T(8,128)S(1)}, u32[]{:S(2)}, u32[]{:S(2)}) collective-permute-start(f32[448,128]{1,0:T(8,128)S(1)} %get-tuple-element.29), channel_id=1, source_target_pairs={{0,2},{2,4},{4,6},{6,8},{8,10},{10,12},{12,14},{3,1},{5,3},{7,5},{... | collective-permute-start | bytes 688136 | tf_op jit(solution)/shard_map/ppermute | solution.py:908
  6.5 6.0 %first.1 = (f32[48,160,128]{2,1,0:T(8,128)S(1)}, f32[48,40,128]{2,1,0:T(8,128)S(1)}, f32[4,160,128]{2,1,0:T(8,128)S(1)}, f32[4,40,128]{2,1,0:T(8,128)S(1)}, f32[...) custom-call(s32[4]{0:T(128)S(4)} %get-tuple-element.23.info, ...), custom_call_target="tpu_custom_call" | custom-call | flops 20000000 | bytes 8000000 | tf_op jit(solution)/shard_map/first/pallas_call | solution.py:729
  12.5 0.0 collective-permute-done.1.ends
  12.5 2.6 %collective-permute-start.2 = (f32[448,128]{1,0:T(8,128)S(1)}, f32[448,128]{1,0:T(8,128)S(1)}, u32[]{:S(2)}, u32[]{:S(2)}) collective-permute-start(f32[448,128]{1,0:T(8,128)S(1)} %follow.1.arrived), channel_id=1, source_target_pairs={{0,1},{1,0},{2,3},{3,2},{4,5},{5,4},{6,7},{7,6},{8,9},{9,8},{10,11... | collective-permute-start | bytes 688136 | tf_op jit(solution)/shard_map/ppermute | solution.py:911
  15.1 2.5 %second.1 = (f32[48,768]{1,0:T(8,128)}, f32[3,48,768]{2,1,0:T(8,128)}, f32[6,48,768]{2,1,0:T(8,128)}, f32[48,768]{1,0:T(8,128)}) custom-call(s32[4]{0:T(128)S(4)} %get-tuple-element.23.info, f32[48,160,128]{2,1,0:T(8,128)S(1)} %get-tuple-element.36.moved, f32[48,40,128]{2,1,0:T(8,128)S(1)} %get-tuple-element.37.reds, f32[448,128]{1,0:T(8,128)S(1)} %follow.1.arrived), custom_call_target="tpu_custom_call" | custom-call | flops 20000000 | bytes 8000000 | tf_op jit(solution)/shard_map/second/pallas_call | solution.py:745
  17.5 0.0 collective-permute-done.2.passed
  17.5 2.3 %outer.1 = (f32[48,768]{1,0:T(8,128)}, f32[3,48,768]{2,1,0:T(8,128)}, f32[6,48,768]{2,1,0:T(8,128)}, f32[48,768]{1,0:T(8,128)}) custom-call(s32[4]{0:T(128)S(4)} %get-tuple-element.23.info, f32[12,384,128]{2,1,0:T(8,128)S(1)} %get-tuple-element.28.whole, ...), custom_call_target="tpu_custom_call", output_to_operand_aliasing={{0}: (10, {}), {1}: (11, {}), {2}: (12, {}), {3}: (13, {})} | custom-call | tf_op jit(solution)/shard_map/outer/pallas_call | solution.py:874
  (1 shorter events, 0.0 us)
Async XLA Ops:
  2.3 1.9 %collective-permute-start = (f32[512,128]{1,0:T(8,128)S(1)}, f32[512,128]{1,0:T(8,128)S(1)}, u32[]{:S(2)}, u32[]{:S(2)}) collective-permute-start(f32[512,128]{1,0:T(8,128)S(1)} %get-tuple-element.26), channel_id=1, source_target_pairs={{0,1},{1,0},{2,3},{3,2},{4,5},{5,4},{6,7},{7,6},{8,9},{9,8},{10,11... | collective-permute-start | bytes 786440 | tf_op jit(solution)/shard_map/ppermute | solution.py:903
  4.3 8.2 %collective-permute-start.1 = (f32[448,128]{1,0:T(8,128)S(1)}, f32[448,128]{1,0:T(8,128)S(1)}, u32[]{:S(2)}, u32[]{:S(2)}) collective-permute-start(f32[448,128]{1,0:T(8,128)S(1)} %get-tuple-element.29), channel_id=1, source_target_pairs={{0,2},{2,4},{4,6},{6,8},{8,10},{10,12},{12,14},{3,1},{5,3},{7,5},{... | collective-permute-start | bytes 688136 | tf_op jit(solution)/shard_map/ppermute | solution.py:908
  12.5 5.0 %collective-permute-start.2 = (f32[448,128]{1,0:T(8,128)S(1)}, f32[448,128]{1,0:T(8,128)S(1)}, u32[]{:S(2)}, u32[]{:S(2)}) collective-permute-start(f32[448,128]{1,0:T(8,128)S(1)} %follow.1.arrived), channel_id=1, source_target_pairs={{0,1},{1,0},{2,3},{3,2},{4,5},{5,4},{6,7},{7,6},{8,9},{9,8},{10,11... | collective-permute-start | bytes 688136 | tf_op jit(solution)/shard_map/ppermute | solution.py:911
